TPU v7x, 32 devices: a whole 2x2x4 slice. The times are simulated.
32 devices in a mesh: ens: 2 (over x), gx: 16 (over z, y, core).
Axes of the slice: x: 2, y: 2, z: 4, core: 2. Of those that a mesh axis runs over, the one named last changes fastest.
Arguments:
- ocean_vel: float32 [4, 1024, 128], P('ens', 'gx'), parts along dimension 0, may hold values from -3 to 3
- wind_stress: float32 [4, 1024, 128], P('ens', 'gx'), parts along dimension 0, may hold values from -3 to 3
- ice_area: float32 [10, 1024, 128], P('ens', 'gx'), parts along dimension 0, may hold values from 0.16 to 0.2
- ice_thick: float32 [10, 1024, 128], P('ens', 'gx'), parts along dimension 0, may hold values from 0.3 to 4
- block_mask: int32 [512], P(('ens', 'gx')), parts along dimension 0, may hold values 0 or 1
- temp: float32 [32, 1024, 128], P('ens', 'gx'), parts along dimension 0, may hold values from -6 to 6
- kappa: float32 [30, 1024, 128], P('ens', 'gx'), parts along dimension 0, may hold values from 0.1 to 10
Outputs:
- mixed_temp: float32 [32, 1024, 128], P('ens', 'gx'), parts along dimension 0
- ice_velocity: float32 [4, 1024, 128], P('ens', 'gx'), parts along dimension 0
- ice_stress: float32 [4, 1024, 128], P('ens', 'gx'), parts along dimension 0
There are 2 independent parts, one for each index of `ens`. A program takes and returns all parts, laid end to end along the dimension named above; each array names one. Nothing has to cross between parts.
All inputs are finite; a program needn't handle non-finite values. No bound on the sum of `block_mask` on one device may be relied on, other than what follows from the above.
Results may differ from a plain program's by a relative error of at most 0.00002.
Values sent between devices are 32-bit elements; how exact they have to be, the bound alone decides.
A program may use at most 64 MiB of HBM per device.

v0:
```python
import jax
import jax.numpy as jnp
from jax import lax
from jax.sharding import PartitionSpec as P

ITERS = 10


strength_coef = 27.5
hardening = 20.0
delta_floor = 0.01
relax_step = 0.5
water_drag = 1.0


def with_halo(value, sides, width):
    for axis, dim in sides:
        size, length = (lax.axis_size(axis), value.shape[dim])
        up = [(i, (i + 1) % size) for i in range(size)]
        down = [(j, i) for i, j in up]
        last = lax.slice_in_dim(value, length - width, length, axis=dim)
        first = lax.slice_in_dim(value, 0, width, axis=dim)
        before = lax.ppermute(last, axis, up)
        after = lax.ppermute(first, axis, down)
        value = jnp.concatenate([before, value, after], axis=dim)
    return value


def strength_of(areas, thicks):
    total = jnp.sum(areas, 0)
    return (total, strength_coef * jnp.sum(areas * thicks, 0) * jnp.exp(-hardening * (1.0 - total)))


def column_mixing(temp, kappa, source):
    levels = temp.shape[0]
    factors = []
    partial_sol = []
    for level in range(levels):
        k_above = kappa[level - 1] if level > 0 else jnp.zeros_like(temp[0])
        k_below = kappa[level] if level < levels - 1 else jnp.zeros_like(temp[0])
        target = temp[0] + source if level == 0 else temp[level]
        diagonal = 1.0 + k_above + k_below
        if level == 0:
            pivot = diagonal
            solved = target / pivot
        else:
            pivot = diagonal + k_above * factors[-1]
            solved = (target + k_above * partial_sol[-1]) / pivot
        factors.append(-k_below / pivot)
        partial_sol.append(solved)
    result = [partial_sol[-1]]
    for level in range(levels - 2, -1, -1):
        result.append(partial_sol[level] - factors[level] * result[-1])
    return jnp.stack(result[::-1], 0)


def relax_update(velocity, eastern, western, folded, strength, forcing, ocean, weights):
    northern = jnp.concatenate([velocity[..., 1:], folded], -1)
    southern = jnp.concatenate([jnp.zeros_like(velocity[..., :1]), velocity[..., :-1]], -1)
    du_x = 0.5 * (eastern[0] - western[0])
    dv_y = 0.5 * (northern[1] - southern[1])
    du_y = 0.5 * (northern[0] - southern[0])
    dv_x = 0.5 * (eastern[1] - western[1])
    delta = jnp.sqrt(
        (du_x + dv_y) ** 2 + 4.0 * ((du_x - dv_y) ** 2 + (du_y + dv_x) ** 2) + delta_floor
    )
    viscous = strength / (2.0 * delta)
    neighbour_sum = eastern + western + northern + southern
    return (
        weights
        * (velocity + relax_step * (viscous * neighbour_sum + forcing + water_drag * ocean))
        / (1.0 + relax_step * (4.0 * viscous + water_drag))
    )


def relax_span(extended, folded, strength, forcing, ocean, weights):
    return relax_update(
        extended[:, 1:-1],
        extended[:, 2:],
        extended[:, :-2],
        folded,
        strength,
        forcing,
        ocean,
        weights,
    )


def body(ocean_vel, wind_stress, ice_area, ice_thick, block_mask, temp, kappa):
    slots = lax.axis_size("gx")
    here = lax.axis_index("gx")
    local_cols = ocean_vel.shape[1]
    width = local_cols // slots
    total, strength = strength_of(ice_area, ice_thick)
    weights = jnp.repeat(block_mask.astype(jnp.float32), width)[:, None]
    anchor = here * local_cols

    def strip_step(count, velocity):
        extended = with_halo(velocity, (("gx", 1),), 1)
        gathered = lax.all_gather(velocity[:, :, -1], "gx", axis=1, tiled=True)
        folded = lax.dynamic_slice_in_dim(-gathered[:, ::-1], anchor, local_cols, 1)[..., None]
        return relax_span(extended, folded, strength, wind_stress, ocean_vel, weights)

    velocity_out = lax.fori_loop(0, ITERS, strip_step, ocean_vel * weights)
    stress_out = water_drag * total * (velocity_out - ocean_vel) * weights
    source = stress_out[0] * ocean_vel[0] + stress_out[1] * ocean_vel[1]
    mixed = column_mixing(temp, kappa, source)
    return (mixed, velocity_out, stress_out)


def solution(mesh):
    placed = (
        P("ens", "gx", None),
        P("ens", "gx", None),
        P("ens", "gx", None),
        P("ens", "gx", None),
        P(("ens", "gx")),
        P("ens", "gx", None),
        P("ens", "gx", None),
    )
    return jax.shard_map(
        body,
        mesh=mesh,
        in_specs=placed,
        out_specs=(P("ens", "gx", None), P("ens", "gx", None), P("ens", "gx", None)),
        check_vma=False,
    )
```

profile of v0, /device:TPU:0, one launch (start us, length us, event | category | flops | bytes accessed | tf_op | source)
XLA Modules:
  0.0 292.7 jit_solution(12237821777383596845)
XLA Ops:
  0.6 0.7 convert_element_type.3
  1.5 0.9 broadcast_multiply_fusion
  2.4 1.0 multiply_reduce_fusion
  3.4 286.0 %while.13 = (s32[]{:T(128)}, f32[2,64,128]{2,1,0:T(8,128)S(1)}, f32[64,128]{1,0:T(8,128)S(1)}, s32[]{:T(128)}, f32[2,64,128]{2,1,0:T(8,128)}, /*index=5*/f32[2,6...) while((s32[]{:T(128)}, f32[2,64,128]{2,1,0:T(8,128)S(1)}, f32[64,128]{1,0:T(8,128)S(1)}, ...), condition=%wide.region_3.0_spmd.clone, body=%wide.region_2.0_spmd.clone.sunk | while | flops 417922 | bytes 2107189 | solution.py:104
  3.5 0.5 collective-permute-start
  4.0 5.1 %collective-permute-start.1 = (f32[2,1,128]{2,1,0:T(1,128)S(1)}, f32[2,1,128]{2,1,0:T(1,128)S(1)}, u32[]{:S(2)}, u32[]{:S(2)}) collective-permute-start(f32[2,1,128]{2,1,0:T(1,128)S(1)} %get-tuple-element.245), channel_id=1, source_target_pairs={{1,0},{2,1},{3,2},{4,3},{5,4},{6,5},{7,6},{8,7},{9,8},{10,9},{11,1... | collective-permute-start | bytes 3080 | tf_op jit(solution)/shard_map/while/body/eval_jaxpr/ppermute | solution.py:24
  9.1 2.6 copy.36
  11.8 1.0 slice.634
  12.8 20.8 %all-gather.3 = f32[2,1024,1]{0,2,1:T(1,128)S(1)} all-gather(f32[2,64,1]{0,2,1:T(1,128)S(1)} %slice.634), channel_id=2, replica_groups=mesh['ens'=2,'gx'=16] {'gx'}, dimensions={1}, use_global_device_ids=true | all-gather | bytes 8704 | tf_op jit(solution)/shard_map/while/body/eval_jaxpr/all_gather | solution.py:100
  33.8 0.5 copy.37
  34.9 0.4 collective-permute-start
  35.3 4.1 %collective-permute-start.1 = (f32[2,1,128]{2,1,0:T(1,128)S(1)}, f32[2,1,128]{2,1,0:T(1,128)S(1)}, u32[]{:S(2)}, u32[]{:S(2)}) collective-permute-start(f32[2,1,128]{2,1,0:T(1,128)S(1)} %get-tuple-element.245), channel_id=1, source_target_pairs={{1,0},{2,1},{3,2},{4,3},{5,4},{6,5},{7,6},{8,7},{9,8},{10,9},{11,1... | collective-permute-start | bytes 3080 | tf_op jit(solution)/shard_map/while/body/eval_jaxpr/ppermute | solution.py:24
  39.4 2.6 copy.36
  42.1 1.0 slice.634
  43.0 18.7 %all-gather.3 = f32[2,1024,1]{0,2,1:T(1,128)S(1)} all-gather(f32[2,64,1]{0,2,1:T(1,128)S(1)} %slice.634), channel_id=2, replica_groups=mesh['ens'=2,'gx'=16] {'gx'}, dimensions={1}, use_global_device_ids=true | all-gather | bytes 8704 | tf_op jit(solution)/shard_map/while/body/eval_jaxpr/all_gather | solution.py:100
  62.0 0.5 copy.37
  63.1 0.4 collective-permute-start
  63.5 4.1 %collective-permute-start.1 = (f32[2,1,128]{2,1,0:T(1,128)S(1)}, f32[2,1,128]{2,1,0:T(1,128)S(1)}, u32[]{:S(2)}, u32[]{:S(2)}) collective-permute-start(f32[2,1,128]{2,1,0:T(1,128)S(1)} %get-tuple-element.245), channel_id=1, source_target_pairs={{1,0},{2,1},{3,2},{4,3},{5,4},{6,5},{7,6},{8,7},{9,8},{10,9},{11,1... | collective-permute-start | bytes 3080 | tf_op jit(solution)/shard_map/while/body/eval_jaxpr/ppermute | solution.py:24
  67.6 2.6 copy.36
  70.3 1.0 slice.634
  71.2 18.8 %all-gather.3 = f32[2,1024,1]{0,2,1:T(1,128)S(1)} all-gather(f32[2,64,1]{0,2,1:T(1,128)S(1)} %slice.634), channel_id=2, replica_groups=mesh['ens'=2,'gx'=16] {'gx'}, dimensions={1}, use_global_device_ids=true | all-gather | bytes 8704 | tf_op jit(solution)/shard_map/while/body/eval_jaxpr/all_gather | solution.py:100
  90.2 0.5 copy.37
  91.3 0.4 collective-permute-start
  91.7 4.1 %collective-permute-start.1 = (f32[2,1,128]{2,1,0:T(1,128)S(1)}, f32[2,1,128]{2,1,0:T(1,128)S(1)}, u32[]{:S(2)}, u32[]{:S(2)}) collective-permute-start(f32[2,1,128]{2,1,0:T(1,128)S(1)} %get-tuple-element.245), channel_id=1, source_target_pairs={{1,0},{2,1},{3,2},{4,3},{5,4},{6,5},{7,6},{8,7},{9,8},{10,9},{11,1... | collective-permute-start | bytes 3080 | tf_op jit(solution)/shard_map/while/body/eval_jaxpr/ppermute | solution.py:24
  95.8 2.6 copy.36
  98.5 1.0 slice.634
  99.5 18.8 %all-gather.3 = f32[2,1024,1]{0,2,1:T(1,128)S(1)} all-gather(f32[2,64,1]{0,2,1:T(1,128)S(1)} %slice.634), channel_id=2, replica_groups=mesh['ens'=2,'gx'=16] {'gx'}, dimensions={1}, use_global_device_ids=true | all-gather | bytes 8704 | tf_op jit(solution)/shard_map/while/body/eval_jaxpr/all_gather | solution.py:100
  118.6 0.5 copy.37
  119.6 0.4 collective-permute-start
  120.0 4.1 %collective-permute-start.1 = (f32[2,1,128]{2,1,0:T(1,128)S(1)}, f32[2,1,128]{2,1,0:T(1,128)S(1)}, u32[]{:S(2)}, u32[]{:S(2)}) collective-permute-start(f32[2,1,128]{2,1,0:T(1,128)S(1)} %get-tuple-element.245), channel_id=1, source_target_pairs={{1,0},{2,1},{3,2},{4,3},{5,4},{6,5},{7,6},{8,7},{9,8},{10,9},{11,1... | collective-permute-start | bytes 3080 | tf_op jit(solution)/shard_map/while/body/eval_jaxpr/ppermute | solution.py:24
  124.1 2.6 copy.36
  126.8 1.0 slice.634
  127.8 18.8 %all-gather.3 = f32[2,1024,1]{0,2,1:T(1,128)S(1)} all-gather(f32[2,64,1]{0,2,1:T(1,128)S(1)} %slice.634), channel_id=2, replica_groups=mesh['ens'=2,'gx'=16] {'gx'}, dimensions={1}, use_global_device_ids=true | all-gather | bytes 8704 | tf_op jit(solution)/shard_map/while/body/eval_jaxpr/all_gather | solution.py:100
  146.9 0.5 copy.37
  148.0 0.4 collective-permute-start
  148.4 4.1 %collective-permute-start.1 = (f32[2,1,128]{2,1,0:T(1,128)S(1)}, f32[2,1,128]{2,1,0:T(1,128)S(1)}, u32[]{:S(2)}, u32[]{:S(2)}) collective-permute-start(f32[2,1,128]{2,1,0:T(1,128)S(1)} %get-tuple-element.245), channel_id=1, source_target_pairs={{1,0},{2,1},{3,2},{4,3},{5,4},{6,5},{7,6},{8,7},{9,8},{10,9},{11,1... | collective-permute-start | bytes 3080 | tf_op jit(solution)/shard_map/while/body/eval_jaxpr/ppermute | solution.py:24
  152.5 2.6 copy.36
  155.2 1.0 slice.634
  156.2 18.8 %all-gather.3 = f32[2,1024,1]{0,2,1:T(1,128)S(1)} all-gather(f32[2,64,1]{0,2,1:T(1,128)S(1)} %slice.634), channel_id=2, replica_groups=mesh['ens'=2,'gx'=16] {'gx'}, dimensions={1}, use_global_device_ids=true | all-gather | bytes 8704 | tf_op jit(solution)/shard_map/while/body/eval_jaxpr/all_gather | solution.py:100
  175.2 0.5 copy.37
  176.3 0.4 collective-permute-start
  176.7 4.1 %collective-permute-start.1 = (f32[2,1,128]{2,1,0:T(1,128)S(1)}, f32[2,1,128]{2,1,0:T(1,128)S(1)}, u32[]{:S(2)}, u32[]{:S(2)}) collective-permute-start(f32[2,1,128]{2,1,0:T(1,128)S(1)} %get-tuple-element.245), channel_id=1, source_target_pairs={{1,0},{2,1},{3,2},{4,3},{5,4},{6,5},{7,6},{8,7},{9,8},{10,9},{11,1... | collective-permute-start | bytes 3080 | tf_op jit(solution)/shard_map/while/body/eval_jaxpr/ppermute | solution.py:24
  180.8 2.6 copy.36
  183.5 1.0 slice.634
  184.5 18.8 %all-gather.3 = f32[2,1024,1]{0,2,1:T(1,128)S(1)} all-gather(f32[2,64,1]{0,2,1:T(1,128)S(1)} %slice.634), channel_id=2, replica_groups=mesh['ens'=2,'gx'=16] {'gx'}, dimensions={1}, use_global_device_ids=true | all-gather | bytes 8704 | tf_op jit(solution)/shard_map/while/body/eval_jaxpr/all_gather | solution.py:100
  203.5 0.5 copy.37
  205.0 4.1 %collective-permute-start.1 = (f32[2,1,128]{2,1,0:T(1,128)S(1)}, f32[2,1,128]{2,1,0:T(1,128)S(1)}, u32[]{:S(2)}, u32[]{:S(2)}) collective-permute-start(f32[2,1,128]{2,1,0:T(1,128)S(1)} %get-tuple-element.245), channel_id=1, source_target_pairs={{1,0},{2,1},{3,2},{4,3},{5,4},{6,5},{7,6},{8,7},{9,8},{10,9},{11,1... | collective-permute-start | bytes 3080 | tf_op jit(solution)/shard_map/while/body/eval_jaxpr/ppermute | solution.py:24
  209.1 2.6 copy.36
  211.8 1.0 slice.634
  212.8 18.8 %all-gather.3 = f32[2,1024,1]{0,2,1:T(1,128)S(1)} all-gather(f32[2,64,1]{0,2,1:T(1,128)S(1)} %slice.634), channel_id=2, replica_groups=mesh['ens'=2,'gx'=16] {'gx'}, dimensions={1}, use_global_device_ids=true | all-gather | bytes 8704 | tf_op jit(solution)/shard_map/while/body/eval_jaxpr/all_gather | solution.py:100
  231.8 0.5 copy.37
  233.3 4.1 %collective-permute-start.1 = (f32[2,1,128]{2,1,0:T(1,128)S(1)}, f32[2,1,128]{2,1,0:T(1,128)S(1)}, u32[]{:S(2)}, u32[]{:S(2)}) collective-permute-start(f32[2,1,128]{2,1,0:T(1,128)S(1)} %get-tuple-element.245), channel_id=1, source_target_pairs={{1,0},{2,1},{3,2},{4,3},{5,4},{6,5},{7,6},{8,7},{9,8},{10,9},{11,1... | collective-permute-start | bytes 3080 | tf_op jit(solution)/shard_map/while/body/eval_jaxpr/ppermute | solution.py:24
  237.4 2.6 copy.36
  240.1 1.0 slice.634
  241.1 18.8 %all-gather.3 = f32[2,1024,1]{0,2,1:T(1,128)S(1)} all-gather(f32[2,64,1]{0,2,1:T(1,128)S(1)} %slice.634), channel_id=2, replica_groups=mesh['ens'=2,'gx'=16] {'gx'}, dimensions={1}, use_global_device_ids=true | all-gather | bytes 8704 | tf_op jit(solution)/shard_map/while/body/eval_jaxpr/all_gather | solution.py:100
  260.1 0.5 copy.37
  261.6 4.1 %collective-permute-start.1 = (f32[2,1,128]{2,1,0:T(1,128)S(1)}, f32[2,1,128]{2,1,0:T(1,128)S(1)}, u32[]{:S(2)}, u32[]{:S(2)}) collective-permute-start(f32[2,1,128]{2,1,0:T(1,128)S(1)} %get-tuple-element.245), channel_id=1, source_target_pairs={{1,0},{2,1},{3,2},{4,3},{5,4},{6,5},{7,6},{8,7},{9,8},{10,9},{11,1... | collective-permute-start | bytes 3080 | tf_op jit(solution)/shard_map/while/body/eval_jaxpr/ppermute | solution.py:24
  265.7 2.6 copy.36
  268.4 1.0 slice.634
  269.4 18.8 %all-gather.3 = f32[2,1024,1]{0,2,1:T(1,128)S(1)} all-gather(f32[2,64,1]{0,2,1:T(1,128)S(1)} %slice.634), channel_id=2, replica_groups=mesh['ens'=2,'gx'=16] {'gx'}, dimensions={1}, use_global_device_ids=true | all-gather | bytes 8704 | tf_op jit(solution)/shard_map/while/body/eval_jaxpr/all_gather | solution.py:100
  288.4 0.5 copy.37
  289.5 0.9 multiply_multiply_fusion
  290.4 1.0 add_divide_fusion.2
  291.9 0.8 copy-done.6
  (201 shorter events, 9.4 us)
Async XLA Ops:
  3.4 287.0 %copy-start.3 = (f32[15,64,128]{2,1,0:T(8,128)S(1)}, f32[15,64,128]{2,1,0:T(8,128)}, u32[]{:S(2)}) copy-start(f32[15,64,128]{2,1,0:T(8,128)} %param.15) | copy-start | bytes 1474564
  3.4 287.0 %copy-start.4 = (f32[16,64,128]{2,1,0:T(8,128)S(1)}, f32[16,64,128]{2,1,0:T(8,128)}, u32[]{:S(2)}) copy-start(f32[16,64,128]{2,1,0:T(8,128)} %param.14) | copy-start | bytes 1572868
  3.5 31.2 %copy-start = (f32[2,64,128]{2,1,0:T(8,128)S(1)}, f32[2,64,128]{2,1,0:T(8,128)}, u32[]{:S(2)}) copy-start(f32[2,64,128]{2,1,0:T(8,128)} %get-tuple-element.275) | copy-start | bytes 196612 | tf_op jit(solution)/shard_map/while
  3.5 31.2 %copy-start.2 = (f32[2,64,128]{2,1,0:T(8,128)S(1)}, f32[2,64,128]{2,1,0:T(8,128)}, u32[]{:S(2)}) copy-start(f32[2,64,128]{2,1,0:T(8,128)} %get-tuple-element.274) | copy-start | bytes 196612 | tf_op jit(solution)/shard_map/while
  3.5 31.0 %collective-permute-start = (f32[2,1,128]{2,1,0:T(1,128)S(1)}, f32[2,1,128]{2,1,0:T(1,128)S(1)}, u32[]{:S(2)}, u32[]{:S(2)}) collective-permute-start(f32[2,1,128]{2,1,0:T(1,128)S(1)} %get-tuple-element.244), channel_id=1, source_target_pairs={{0,1},{1,2},{2,3},{3,4},{4,5},{5,6},{6,7},{7,8},{8,9},{9,10},{10,1... | collective-permute-start | bytes 3080 | tf_op jit(solution)/shard_map/while/body/eval_jaxpr/ppermute | solution.py:23
  4.0 30.4 %collective-permute-start.1 = (f32[2,1,128]{2,1,0:T(1,128)S(1)}, f32[2,1,128]{2,1,0:T(1,128)S(1)}, u32[]{:S(2)}, u32[]{:S(2)}) collective-permute-start(f32[2,1,128]{2,1,0:T(1,128)S(1)} %get-tuple-element.245), channel_id=1, source_target_pairs={{1,0},{2,1},{3,2},{4,3},{5,4},{6,5},{7,6},{8,7},{9,8},{10,9},{11,1... | collective-permute-start | bytes 3080 | tf_op jit(solution)/shard_map/while/body/eval_jaxpr/ppermute | solution.py:24
  34.8 28.1 %copy-start = (f32[2,64,128]{2,1,0:T(8,128)S(1)}, f32[2,64,128]{2,1,0:T(8,128)}, u32[]{:S(2)}) copy-start(f32[2,64,128]{2,1,0:T(8,128)} %get-tuple-element.275) | copy-start | bytes 196612 | tf_op jit(solution)/shard_map/while
  34.8 28.0 %copy-start.2 = (f32[2,64,128]{2,1,0:T(8,128)S(1)}, f32[2,64,128]{2,1,0:T(8,128)}, u32[]{:S(2)}) copy-start(f32[2,64,128]{2,1,0:T(8,128)} %get-tuple-element.274) | copy-start | bytes 196612 | tf_op jit(solution)/shard_map/while
  34.9 27.8 %collective-permute-start = (f32[2,1,128]{2,1,0:T(1,128)S(1)}, f32[2,1,128]{2,1,0:T(1,128)S(1)}, u32[]{:S(2)}, u32[]{:S(2)}) collective-permute-start(f32[2,1,128]{2,1,0:T(1,128)S(1)} %get-tuple-element.244), channel_id=1, source_target_pairs={{0,1},{1,2},{2,3},{3,4},{4,5},{5,6},{6,7},{7,8},{8,9},{9,10},{10,1... | collective-permute-start | bytes 3080 | tf_op jit(solution)/shard_map/while/body/eval_jaxpr/ppermute | solution.py:23
  35.3 27.4 %collective-permute-start.1 = (f32[2,1,128]{2,1,0:T(1,128)S(1)}, f32[2,1,128]{2,1,0:T(1,128)S(1)}, u32[]{:S(2)}, u32[]{:S(2)}) collective-permute-start(f32[2,1,128]{2,1,0:T(1,128)S(1)} %get-tuple-element.245), channel_id=1, source_target_pairs={{1,0},{2,1},{3,2},{4,3},{5,4},{6,5},{7,6},{8,7},{9,8},{10,9},{11,1... | collective-permute-start | bytes 3080 | tf_op jit(solution)/shard_map/while/body/eval_jaxpr/ppermute | solution.py:24
  63.0 28.1 %copy-start = (f32[2,64,128]{2,1,0:T(8,128)S(1)}, f32[2,64,128]{2,1,0:T(8,128)}, u32[]{:S(2)}) copy-start(f32[2,64,128]{2,1,0:T(8,128)} %get-tuple-element.275) | copy-start | bytes 196612 | tf_op jit(solution)/shard_map/while
  63.0 28.1 %copy-start.2 = (f32[2,64,128]{2,1,0:T(8,128)S(1)}, f32[2,64,128]{2,1,0:T(8,128)}, u32[]{:S(2)}) copy-start(f32[2,64,128]{2,1,0:T(8,128)} %get-tuple-element.274) | copy-start | bytes 196612 | tf_op jit(solution)/shard_map/while
  63.1 27.9 %collective-permute-start = (f32[2,1,128]{2,1,0:T(1,128)S(1)}, f32[2,1,128]{2,1,0:T(1,128)S(1)}, u32[]{:S(2)}, u32[]{:S(2)}) collective-permute-start(f32[2,1,128]{2,1,0:T(1,128)S(1)} %get-tuple-element.244), channel_id=1, source_target_pairs={{0,1},{1,2},{2,3},{3,4},{4,5},{5,6},{6,7},{7,8},{8,9},{9,10},{10,1... | collective-permute-start | bytes 3080 | tf_op jit(solution)/shard_map/while/body/eval_jaxpr/ppermute | solution.py:23
  63.5 27.5 %collective-permute-start.1 = (f32[2,1,128]{2,1,0:T(1,128)S(1)}, f32[2,1,128]{2,1,0:T(1,128)S(1)}, u32[]{:S(2)}, u32[]{:S(2)}) collective-permute-start(f32[2,1,128]{2,1,0:T(1,128)S(1)} %get-tuple-element.245), channel_id=1, source_target_pairs={{1,0},{2,1},{3,2},{4,3},{5,4},{6,5},{7,6},{8,7},{9,8},{10,9},{11,1... | collective-permute-start | bytes 3080 | tf_op jit(solution)/shard_map/while/body/eval_jaxpr/ppermute | solution.py:24
  91.3 28.2 %copy-start = (f32[2,64,128]{2,1,0:T(8,128)S(1)}, f32[2,64,128]{2,1,0:T(8,128)}, u32[]{:S(2)}) copy-start(f32[2,64,128]{2,1,0:T(8,128)} %get-tuple-element.275) | copy-start | bytes 196612 | tf_op jit(solution)/shard_map/while
  91.3 28.2 %copy-start.2 = (f32[2,64,128]{2,1,0:T(8,128)S(1)}, f32[2,64,128]{2,1,0:T(8,128)}, u32[]{:S(2)}) copy-start(f32[2,64,128]{2,1,0:T(8,128)} %get-tuple-element.274) | copy-start | bytes 196612 | tf_op jit(solution)/shard_map/while
  91.3 28.0 %collective-permute-start = (f32[2,1,128]{2,1,0:T(1,128)S(1)}, f32[2,1,128]{2,1,0:T(1,128)S(1)}, u32[]{:S(2)}, u32[]{:S(2)}) collective-permute-start(f32[2,1,128]{2,1,0:T(1,128)S(1)} %get-tuple-element.244), channel_id=1, source_target_pairs={{0,1},{1,2},{2,3},{3,4},{4,5},{5,6},{6,7},{7,8},{8,9},{9,10},{10,1... | collective-permute-start | bytes 3080 | tf_op jit(solution)/shard_map/while/body/eval_jaxpr/ppermute | solution.py:23
  91.7 27.5 %collective-permute-start.1 = (f32[2,1,128]{2,1,0:T(1,128)S(1)}, f32[2,1,128]{2,1,0:T(1,128)S(1)}, u32[]{:S(2)}, u32[]{:S(2)}) collective-permute-start(f32[2,1,128]{2,1,0:T(1,128)S(1)} %get-tuple-element.245), channel_id=1, source_target_pairs={{1,0},{2,1},{3,2},{4,3},{5,4},{6,5},{7,6},{8,7},{9,8},{10,9},{11,1... | collective-permute-start | bytes 3080 | tf_op jit(solution)/shard_map/while/body/eval_jaxpr/ppermute | solution.py:24
  119.6 28.2 %copy-start = (f32[2,64,128]{2,1,0:T(8,128)S(1)}, f32[2,64,128]{2,1,0:T(8,128)}, u32[]{:S(2)}) copy-start(f32[2,64,128]{2,1,0:T(8,128)} %get-tuple-element.275) | copy-start | bytes 196612 | tf_op jit(solution)/shard_map/while
  119.6 28.2 %copy-start.2 = (f32[2,64,128]{2,1,0:T(8,128)S(1)}, f32[2,64,128]{2,1,0:T(8,128)}, u32[]{:S(2)}) copy-start(f32[2,64,128]{2,1,0:T(8,128)} %get-tuple-element.274) | copy-start | bytes 196612 | tf_op jit(solution)/shard_map/while
  119.6 28.0 %collective-permute-start = (f32[2,1,128]{2,1,0:T(1,128)S(1)}, f32[2,1,128]{2,1,0:T(1,128)S(1)}, u32[]{:S(2)}, u32[]{:S(2)}) collective-permute-start(f32[2,1,128]{2,1,0:T(1,128)S(1)} %get-tuple-element.244), channel_id=1, source_target_pairs={{0,1},{1,2},{2,3},{3,4},{4,5},{5,6},{6,7},{7,8},{8,9},{9,10},{10,1... | collective-permute-start | bytes 3080 | tf_op jit(solution)/shard_map/while/body/eval_jaxpr/ppermute | solution.py:23
  120.0 27.5 %collective-permute-start.1 = (f32[2,1,128]{2,1,0:T(1,128)S(1)}, f32[2,1,128]{2,1,0:T(1,128)S(1)}, u32[]{:S(2)}, u32[]{:S(2)}) collective-permute-start(f32[2,1,128]{2,1,0:T(1,128)S(1)} %get-tuple-element.245), channel_id=1, source_target_pairs={{1,0},{2,1},{3,2},{4,3},{5,4},{6,5},{7,6},{8,7},{9,8},{10,9},{11,1... | collective-permute-start | bytes 3080 | tf_op jit(solution)/shard_map/while/body/eval_jaxpr/ppermute | solution.py:24
  147.9 28.2 %copy-start = (f32[2,64,128]{2,1,0:T(8,128)S(1)}, f32[2,64,128]{2,1,0:T(8,128)}, u32[]{:S(2)}) copy-start(f32[2,64,128]{2,1,0:T(8,128)} %get-tuple-element.275) | copy-start | bytes 196612 | tf_op jit(solution)/shard_map/while
  147.9 28.2 %copy-start.2 = (f32[2,64,128]{2,1,0:T(8,128)S(1)}, f32[2,64,128]{2,1,0:T(8,128)}, u32[]{:S(2)}) copy-start(f32[2,64,128]{2,1,0:T(8,128)} %get-tuple-element.274) | copy-start | bytes 196612 | tf_op jit(solution)/shard_map/while
  148.0 28.0 %collective-permute-start = (f32[2,1,128]{2,1,0:T(1,128)S(1)}, f32[2,1,128]{2,1,0:T(1,128)S(1)}, u32[]{:S(2)}, u32[]{:S(2)}) collective-permute-start(f32[2,1,128]{2,1,0:T(1,128)S(1)} %get-tuple-element.244), channel_id=1, source_target_pairs={{0,1},{1,2},{2,3},{3,4},{4,5},{5,6},{6,7},{7,8},{8,9},{9,10},{10,1... | collective-permute-start | bytes 3080 | tf_op jit(solution)/shard_map/while/body/eval_jaxpr/ppermute | solution.py:23
  148.4 27.5 %collective-permute-start.1 = (f32[2,1,128]{2,1,0:T(1,128)S(1)}, f32[2,1,128]{2,1,0:T(1,128)S(1)}, u32[]{:S(2)}, u32[]{:S(2)}) collective-permute-start(f32[2,1,128]{2,1,0:T(1,128)S(1)} %get-tuple-element.245), channel_id=1, source_target_pairs={{1,0},{2,1},{3,2},{4,3},{5,4},{6,5},{7,6},{8,7},{9,8},{10,9},{11,1... | collective-permute-start | bytes 3080 | tf_op jit(solution)/shard_map/while/body/eval_jaxpr/ppermute | solution.py:24
  176.2 28.2 %copy-start = (f32[2,64,128]{2,1,0:T(8,128)S(1)}, f32[2,64,128]{2,1,0:T(8,128)}, u32[]{:S(2)}) copy-start(f32[2,64,128]{2,1,0:T(8,128)} %get-tuple-element.275) | copy-start | bytes 196612 | tf_op jit(solution)/shard_map/while
  176.2 28.2 %copy-start.2 = (f32[2,64,128]{2,1,0:T(8,128)S(1)}, f32[2,64,128]{2,1,0:T(8,128)}, u32[]{:S(2)}) copy-start(f32[2,64,128]{2,1,0:T(8,128)} %get-tuple-element.274) | copy-start | bytes 196612 | tf_op jit(solution)/shard_map/while
  176.3 28.0 %collective-permute-start = (f32[2,1,128]{2,1,0:T(1,128)S(1)}, f32[2,1,128]{2,1,0:T(1,128)S(1)}, u32[]{:S(2)}, u32[]{:S(2)}) collective-permute-start(f32[2,1,128]{2,1,0:T(1,128)S(1)} %get-tuple-element.244), channel_id=1, source_target_pairs={{0,1},{1,2},{2,3},{3,4},{4,5},{5,6},{6,7},{7,8},{8,9},{9,10},{10,1... | collective-permute-start | bytes 3080 | tf_op jit(solution)/shard_map/while/body/eval_jaxpr/ppermute | solution.py:23
  176.7 27.5 %collective-permute-start.1 = (f32[2,1,128]{2,1,0:T(1,128)S(1)}, f32[2,1,128]{2,1,0:T(1,128)S(1)}, u32[]{:S(2)}, u32[]{:S(2)}) collective-permute-start(f32[2,1,128]{2,1,0:T(1,128)S(1)} %get-tuple-element.245), channel_id=1, source_target_pairs={{1,0},{2,1},{3,2},{4,3},{5,4},{6,5},{7,6},{8,7},{9,8},{10,9},{11,1... | collective-permute-start | bytes 3080 | tf_op jit(solution)/shard_map/while/body/eval_jaxpr/ppermute | solution.py:24
  204.5 28.2 %copy-start = (f32[2,64,128]{2,1,0:T(8,128)S(1)}, f32[2,64,128]{2,1,0:T(8,128)}, u32[]{:S(2)}) copy-start(f32[2,64,128]{2,1,0:T(8,128)} %get-tuple-element.275) | copy-start | bytes 196612 | tf_op jit(solution)/shard_map/while
  204.5 28.2 %copy-start.2 = (f32[2,64,128]{2,1,0:T(8,128)S(1)}, f32[2,64,128]{2,1,0:T(8,128)}, u32[]{:S(2)}) copy-start(f32[2,64,128]{2,1,0:T(8,128)} %get-tuple-element.274) | copy-start | bytes 196612 | tf_op jit(solution)/shard_map/while
  204.6 28.0 %collective-permute-start = (f32[2,1,128]{2,1,0:T(1,128)S(1)}, f32[2,1,128]{2,1,0:T(1,128)S(1)}, u32[]{:S(2)}, u32[]{:S(2)}) collective-permute-start(f32[2,1,128]{2,1,0:T(1,128)S(1)} %get-tuple-element.244), channel_id=1, source_target_pairs={{0,1},{1,2},{2,3},{3,4},{4,5},{5,6},{6,7},{7,8},{8,9},{9,10},{10,1... | collective-permute-start | bytes 3080 | tf_op jit(solution)/shard_map/while/body/eval_jaxpr/ppermute | solution.py:23
  205.0 27.5 %collective-permute-start.1 = (f32[2,1,128]{2,1,0:T(1,128)S(1)}, f32[2,1,128]{2,1,0:T(1,128)S(1)}, u32[]{:S(2)}, u32[]{:S(2)}) collective-permute-start(f32[2,1,128]{2,1,0:T(1,128)S(1)} %get-tuple-element.245), channel_id=1, source_target_pairs={{1,0},{2,1},{3,2},{4,3},{5,4},{6,5},{7,6},{8,7},{9,8},{10,9},{11,1... | collective-permute-start | bytes 3080 | tf_op jit(solution)/shard_map/while/body/eval_jaxpr/ppermute | solution.py:24
  232.8 28.2 %copy-start = (f32[2,64,128]{2,1,0:T(8,128)S(1)}, f32[2,64,128]{2,1,0:T(8,128)}, u32[]{:S(2)}) copy-start(f32[2,64,128]{2,1,0:T(8,128)} %get-tuple-element.275) | copy-start | bytes 196612 | tf_op jit(solution)/shard_map/while
  232.9 28.2 %copy-start.2 = (f32[2,64,128]{2,1,0:T(8,128)S(1)}, f32[2,64,128]{2,1,0:T(8,128)}, u32[]{:S(2)}) copy-start(f32[2,64,128]{2,1,0:T(8,128)} %get-tuple-element.274) | copy-start | bytes 196612 | tf_op jit(solution)/shard_map/while
  232.9 28.0 %collective-permute-start = (f32[2,1,128]{2,1,0:T(1,128)S(1)}, f32[2,1,128]{2,1,0:T(1,128)S(1)}, u32[]{:S(2)}, u32[]{:S(2)}) collective-permute-start(f32[2,1,128]{2,1,0:T(1,128)S(1)} %get-tuple-element.244), channel_id=1, source_target_pairs={{0,1},{1,2},{2,3},{3,4},{4,5},{5,6},{6,7},{7,8},{8,9},{9,10},{10,1... | collective-permute-start | bytes 3080 | tf_op jit(solution)/shard_map/while/body/eval_jaxpr/ppermute | solution.py:23
  233.3 27.5 %collective-permute-start.1 = (f32[2,1,128]{2,1,0:T(1,128)S(1)}, f32[2,1,128]{2,1,0:T(1,128)S(1)}, u32[]{:S(2)}, u32[]{:S(2)}) collective-permute-start(f32[2,1,128]{2,1,0:T(1,128)S(1)} %get-tuple-element.245), channel_id=1, source_target_pairs={{1,0},{2,1},{3,2},{4,3},{5,4},{6,5},{7,6},{8,7},{9,8},{10,9},{11,1... | collective-permute-start | bytes 3080 | tf_op jit(solution)/shard_map/while/body/eval_jaxpr/ppermute | solution.py:24
  261.2 28.2 %copy-start = (f32[2,64,128]{2,1,0:T(8,128)S(1)}, f32[2,64,128]{2,1,0:T(8,128)}, u32[]{:S(2)}) copy-start(f32[2,64,128]{2,1,0:T(8,128)} %get-tuple-element.275) | copy-start | bytes 196612 | tf_op jit(solution)/shard_map/while
  261.2 28.2 %copy-start.2 = (f32[2,64,128]{2,1,0:T(8,128)S(1)}, f32[2,64,128]{2,1,0:T(8,128)}, u32[]{:S(2)}) copy-start(f32[2,64,128]{2,1,0:T(8,128)} %get-tuple-element.274) | copy-start | bytes 196612 | tf_op jit(solution)/shard_map/while
  261.2 28.0 %collective-permute-start = (f32[2,1,128]{2,1,0:T(1,128)S(1)}, f32[2,1,128]{2,1,0:T(1,128)S(1)}, u32[]{:S(2)}, u32[]{:S(2)}) collective-permute-start(f32[2,1,128]{2,1,0:T(1,128)S(1)} %get-tuple-element.244), channel_id=1, source_target_pairs={{0,1},{1,2},{2,3},{3,4},{4,5},{5,6},{6,7},{7,8},{8,9},{9,10},{10,1... | collective-permute-start | bytes 3080 | tf_op jit(solution)/shard_map/while/body/eval_jaxpr/ppermute | solution.py:23
  261.6 27.5 %collective-permute-start.1 = (f32[2,1,128]{2,1,0:T(1,128)S(1)}, f32[2,1,128]{2,1,0:T(1,128)S(1)}, u32[]{:S(2)}, u32[]{:S(2)}) collective-permute-start(f32[2,1,128]{2,1,0:T(1,128)S(1)} %get-tuple-element.245), channel_id=1, source_target_pairs={{1,0},{2,1},{3,2},{4,3},{5,4},{6,5},{7,6},{8,7},{9,8},{10,9},{11,1... | collective-permute-start | bytes 3080 | tf_op jit(solution)/shard_map/while/body/eval_jaxpr/ppermute | solution.py:24
  289.5 2.4 copy-start.1
  290.4 1.4 copy-start.5
  291.9 0.8 copy-start.6
where the time goes:
time: 293 us
  blocking collectives  190 us (65%)
  local copies, waits for them, and re-layouts  47.2 us (16%)
  starting transfers between devices  46 us (16%)
  other arithmetic  7.52 us (3%)
    all_gather x10, blocking collectives, strip_step(): gathered = lax.all_gather(velocity[:, :, -1], 'gx', axis=1, tiled=True)  190 us
    ppermute x10, starting transfers between devices, with_halo(): after = lax.ppermute(first, axis, down)  41.9 us
    while x70, local copies, waits for them, and re-layouts  26.5 us
    slice x10, local copies, waits for them, and re-layouts, strip_step(): gathered = lax.all_gather(velocity[:, :, -1], 'gx', axis=1, tiled=True)  9.87 us
  transfers between devices with their start and end apart: 20, of which 0 were waited for; matrix products, arithmetic and copies ran while one was open for 16% of the time, Pallas kernels for 0%

commit v1 on v0

v1 whole, which is shorter than its diff:
```python
import functools

import jax
import jax.numpy as jnp
from jax import lax
from jax.experimental import pallas as pl
from jax.experimental.pallas import tpu as pltpu
from jax.sharding import PartitionSpec as P

ITERS = 10
HALO = 16
FIELDS = 5
MESH = pl.DeviceIdType.MESH
HIGH = lax.Precision.HIGHEST


def advance(u, v, eastern, western, northern, southern, fu, fv, half_strength):
    (eu, ev), (wu, wv), (nu, nv), (su, sv) = eastern, western, northern, southern
    du_x = eu - wu
    dv_y = nv - sv
    shear = (nu - su) + (ev - wv)
    plus = du_x + dv_y
    minus = du_x - dv_y
    squared = plus * plus + (4.0 * (minus * minus + shear * shear) + 0.04)
    half_zeta = half_strength * lax.rsqrt(squared)
    scale = 1.0 / (1.5 + 4.0 * half_zeta)
    new_u = (u + half_zeta * ((eu + wu) + (nu + su)) + fu) * scale
    new_v = (v + half_zeta * ((ev + wv) + (nv + sv)) + fv) * scale
    return new_u, new_v


def kernel(
    slots, mask, ocean_hbm, wind_hbm, area_hbm, thick_hbm, temp_hbm, kappa_hbm,
    mixed_hbm, velocity_hbm, stress_hbm,
    ocean, wind, area, thick, temp, kappa, fields, strips, mirrored, arrived,
    total_ref, weight_ref, first_ref, rows_ref, velocity, stress,
    in_sem, out_sem, send_sem, recv_sem,
):
    n = ocean.shape[1]
    levels = temp.shape[0]
    width = n // mask.shape[0]
    ens, here = lax.axis_index("ens"), lax.axis_index("gx")
    east = lax.rem(here + 1, slots)
    west = lax.rem(here + slots - 1, slots)
    partner = slots - 1 - here
    partner_east = lax.rem(partner + 1, slots)
    partner_west = lax.rem(partner + slots - 1, slots)

    loads = [
        pltpu.make_async_copy(src, dst, in_sem.at[k])
        for k, (src, dst) in enumerate([
            (area_hbm, area), (thick_hbm, thick), (ocean_hbm, ocean),
            (wind_hbm, wind), (kappa_hbm, kappa), (temp_hbm, temp),
        ])
    ]
    for load in loads:
        load.start()

    barrier = pltpu.get_barrier_semaphore()
    for target in (east, west, partner):
        pl.semaphore_signal(barrier, inc=1, device_id=(ens, target), device_id_type=MESH)

    @pl.when(partner_east != here)
    def _():
        pl.semaphore_signal(barrier, inc=1, device_id=(ens, partner_east), device_id_type=MESH)

    @pl.when(partner_west != here)
    def _():
        pl.semaphore_signal(barrier, inc=1, device_id=(ens, partner_west), device_id_type=MESH)

    for load in loads[:4]:
        load.wait()

    sub = lax.broadcasted_iota(jnp.int32, (8, 128), 0)
    chunks = []
    for start in range(0, n, 8):
        chunk = jnp.zeros((8, 128), jnp.float32)
        for row in range(0, 8, width):
            value = mask[(start + row) // width].astype(jnp.float32)
            chunk = jnp.where(sub >= row, value, chunk)
        chunks.append(chunk)
    weights = jnp.concatenate(chunks, 0)
    weight_ref[...] = weights
    total = area[0]
    volume = area[0] * thick[0]
    for cat in range(1, area.shape[0]):
        total = total + area[cat]
        volume = volume + area[cat] * thick[cat]
    total_ref[...] = total
    half_strength = (13.75 * weights) * volume * jnp.exp(-20.0 * (1.0 - total))
    inner = pl.ds(HALO, n)
    values = []
    for comp in range(2):
        values.append(ocean[comp] * weights)
    for comp in range(2):
        values.append(0.5 * (wind[comp] + ocean[comp]) * weights)
    values.append(half_strength)

    pick_row = lax.broadcasted_iota(jnp.int32, (2 * HALO, 128), 0)
    pick_lane = lax.broadcasted_iota(jnp.int32, (2 * HALO, 128), 1)
    wanted = jnp.where(pick_row < HALO, 128 - HALO + pick_row, 127 + HALO - pick_row)
    pick = jnp.where(pick_lane == wanted, 1.0, 0.0).astype(jnp.float32)
    place_col = lax.broadcasted_iota(jnp.int32, (n, 2 * n), 0)
    place_lane = lax.broadcasted_iota(jnp.int32, (n, 2 * n), 1)
    place_lane = jnp.where(place_lane >= n, place_lane - n, place_lane)
    place = jnp.where(place_lane == place_col, 1.0, 0.0).astype(jnp.float32)
    place_back = jnp.where(n - 1 - place_lane == place_col, 1.0, 0.0).astype(jnp.float32)
    tops = []
    for k in range(FIELDS):
        fields[k, inner, :] = values[k]
        tops.append(lax.dot_general(
            pick, values[k], (((1,), (1,)), ((), ())), precision=HIGH,
            preferred_element_type=jnp.float32))
    forward = jnp.concatenate([top[:HALO] for top in tops], 0)
    backward = jnp.concatenate(
        [(-top[HALO:] if k < 4 else top[HALO:]) for k, top in enumerate(tops)], 0)
    strips[...] = jnp.dot(
        forward, place, precision=HIGH, preferred_element_type=jnp.float32
    ).reshape(FIELDS, HALO, 2 * n)
    mirrored[...] = jnp.dot(
        backward, place_back, precision=HIGH, preferred_element_type=jnp.float32
    ).reshape(FIELDS, HALO, 2 * n)

    others = (partner_east != here).astype(jnp.int32) + (partner_west != here).astype(jnp.int32)
    pl.semaphore_wait(barrier, 3 + others)

    def remote(src, dst, slot, target):
        return pltpu.make_async_remote_copy(
            src_ref=src, dst_ref=dst, send_sem=send_sem.at[slot],
            recv_sem=recv_sem.at[slot], device_id=(ens, target), device_id_type=MESH)

    first, last = pl.ds(HALO, HALO), pl.ds(n, HALO)
    copies = [
        remote(mirrored, arrived.at[2], 2, partner),
        remote(strips, arrived.at[0], 0, east),
        remote(strips, arrived.at[1], 1, west),
        remote(fields.at[:, last, :], fields.at[:, pl.ds(0, HALO), :], 5, east),
        remote(fields.at[:, first, :], fields.at[:, pl.ds(HALO + n, HALO), :], 6, west),
    ]
    to_west = remote(mirrored, arrived.at[3], 3, partner_west)
    to_east = remote(mirrored, arrived.at[4], 4, partner_east)

    @pl.when(partner_west != here)
    def _():
        to_west.start()

    @pl.when(partner_west == here)
    def _():
        arrived[3] = mirrored[...]

    @pl.when(partner_east != here)
    def _():
        to_east.start()

    @pl.when(partner_east == here)
    def _():
        arrived[4] = mirrored[...]

    for copy in copies:
        copy.start()

    for load in loads[4:]:
        load.wait()
    factor = None
    solved = None
    for level in range(levels - 1, -1, -1):
        target = temp[level]
        pivot = 1.0
        if level < levels - 1:
            below = kappa[level]
            pivot = 1.0 + below * (1.0 - factor)
            target = target + below * solved
        if level > 0:
            above = kappa[level - 1]
            inverse = 1.0 / (pivot + above)
            factor = above * inverse
            solved = target * inverse
            if level < levels - 1:
                kappa[level] = carried
            carried = factor
            temp[level] = solved
        else:
            kappa[0] = carried
            inverse = 1.0 / pivot
            first_ref[...] = inverse
            temp[0] = target * inverse

    @pl.when(partner_west != here)
    def _():
        to_west.wait()

    @pl.when(partner_east != here)
    def _():
        to_east.wait()

    for copy in copies:
        copy.wait()

    lane = lax.broadcasted_iota(jnp.int32, (HALO, 2 * n), 1)
    strip = []
    for k in range(FIELDS):
        south = jnp.where(
            lane >= n, strips[k], jnp.where(lane >= n // 2, arrived[0, k], arrived[1, k]))
        north = jnp.where(
            lane >= n, arrived[2, k], jnp.where(lane >= n // 2, arrived[4, k], arrived[3, k]))
        strip.append(jnp.concatenate([south, north], 0))
    u, v, fu, fv, half = strip
    for count in range(ITERS):
        rows_ref[2 * count:2 * count + 1, :] = u[HALO:HALO + 1, :]
        rows_ref[2 * count + 1:2 * count + 2, :] = v[HALO:HALO + 1, :]
        if count < ITERS - 1:
            pairs = [
                [pltpu.roll(w, shift, axis) for w in (u, v)]
                for axis, shift in ((1, 2 * n - 1), (1, 1), (0, 2 * HALO - 1), (0, 1))
            ]
            u, v = advance(u, v, *pairs, fu, fv, half)

    turned = rows_ref[...].T
    crossed = jnp.concatenate([turned[n - HALO:], turned[:HALO]], 0)
    u, v, fu, fv, half = [fields[k] for k in range(FIELDS)]
    for count in range(ITERS):
        if count == 2:
            cut = slice(8, n + 24)
            u, v, fu, fv, half, crossed = [w[cut] for w in (u, v, fu, fv, half, crossed)]
        size = u.shape[0]
        rows = lax.broadcasted_iota(jnp.int32, (size, 128), 1)
        eastern = [pltpu.roll(w, size - 1, 0) for w in (u, v)]
        western = [pltpu.roll(w, 1, 0) for w in (u, v)]
        northern = [
            jnp.where(rows == 127, pltpu.roll(crossed, 127 - 2 * count - comp, 1), pltpu.roll(w, 127, 1))
            for comp, w in enumerate((u, v))
        ]
        southern = [jnp.where(rows == 0, 0.0, pltpu.roll(w, 1, 1)) for w in (u, v)]
        u, v = advance(u, v, eastern, western, northern, southern, fu, fv, half)

    source = jnp.zeros((n, 128), jnp.float32)
    scale = total_ref[...] * weight_ref[...]
    for comp, w in enumerate((u, v)):
        w = w[8:8 + n]
        velocity[comp] = w
        drag = scale * (w - ocean[comp])
        stress[comp] = drag
        source = source + drag * ocean[comp]
    stores = [
        pltpu.make_async_copy(velocity, velocity_hbm, out_sem.at[0]),
        pltpu.make_async_copy(stress, stress_hbm, out_sem.at[1]),
    ]
    for store in stores:
        store.start()
    level_value = temp[0] + first_ref[...] * source
    temp[0] = level_value
    quarter = levels // 4
    for level in range(1, levels):
        level_value = temp[level] + kappa[level - 1] * level_value
        temp[level] = level_value
        if level % quarter == quarter - 1:
            part = pl.ds(level - quarter + 1, quarter)
            store = pltpu.make_async_copy(
                temp.at[part], mixed_hbm.at[part], out_sem.at[2 + level // quarter])
            store.start()
            stores.append(store)
    for store in stores:
        store.wait()


def solution(mesh):
    slots = mesh.shape["gx"]

    def body(ocean_vel, wind_stress, ice_area, ice_thick, block_mask, temp, kappa):
        n, ny = ocean_vel.shape[1:]
        levels, cats = temp.shape[0], ice_area.shape[0]
        any_spec = pl.BlockSpec(memory_space=pl.ANY)
        f32 = jnp.float32
        return pl.pallas_call(
            functools.partial(kernel, slots),
            out_shape=(
                jax.ShapeDtypeStruct(temp.shape, f32),
                jax.ShapeDtypeStruct(ocean_vel.shape, f32),
                jax.ShapeDtypeStruct(ocean_vel.shape, f32),
            ),
            in_specs=[pl.BlockSpec(memory_space=pltpu.SMEM)] + [any_spec] * 6,
            out_specs=(any_spec,) * 3,
            scratch_shapes=[
                pltpu.VMEM((2, n, ny), f32),
                pltpu.VMEM((2, n, ny), f32),
                pltpu.VMEM((cats, n, ny), f32),
                pltpu.VMEM((cats, n, ny), f32),
                pltpu.VMEM((levels, n, ny), f32),
                pltpu.VMEM((levels - 1, n, ny), f32),
                pltpu.VMEM((FIELDS, n + 2 * HALO, ny), f32),
                pltpu.VMEM((FIELDS, HALO, 2 * n), f32),
                pltpu.VMEM((FIELDS, HALO, 2 * n), f32),
                pltpu.VMEM((5, FIELDS, HALO, 2 * n), f32),
                pltpu.VMEM((n, ny), f32),
                pltpu.VMEM((n, ny), f32),
                pltpu.VMEM((n, ny), f32),
                pltpu.VMEM((128, 2 * n), f32),
                pltpu.VMEM((2, n, ny), f32),
                pltpu.VMEM((2, n, ny), f32),
                pltpu.SemaphoreType.DMA((6,)),
                pltpu.SemaphoreType.DMA((6,)),
                pltpu.SemaphoreType.DMA((7,)),
                pltpu.SemaphoreType.DMA((7,)),
            ],
            compiler_params=pltpu.CompilerParams(
                collective_id=0, has_side_effects=True, vmem_limit_bytes=24 * 1024 * 1024),
            name="ice_ocean",
        )(block_mask, ocean_vel, wind_stress, ice_area, ice_thick, temp, kappa)

    split = P("ens", "gx", None)
    return jax.shard_map(
        body,
        mesh=mesh,
        in_specs=(split, split, split, split, P(("ens", "gx")), split, split),
        out_specs=(split, split, split),
        check_vma=False,
    )
```

time: 293 us -> 24.6 us (0.08)
  the two profiles are of different devices: /device:TPU:0 before, /device:TPU:10 now
where the time goes in v1:
time: 24.6 us; the launch traced here: 24.3 us
  Pallas kernels  15.3 us (62%)
  local copies, waits for them, and re-layouts  8.28 us (34%)
  between operations  0.66 us (3%)
    pallas_call x1, Pallas kernels, body(): pl.pallas_call(functools.partial(kernel, slots), out_shape=(jax.ShapeDtyp...  15.3 us
    unnamed x17, local copies, waits for them, and re-layouts  8.28 us

profile of v1, /device:TPU:10, one launch (start us, length us, event | category | flops | bytes accessed | tf_op | source)
XLA Modules:
  0.0 24.3 jit_solution(4667378398615783103)
XLA Ops:
  0.6 0.0 copy-start
  0.6 1.0 %copy-done = f32[16,64,128]{2,1,0:T(8,128)S(1)} copy-done((f32[16,64,128]{2,1,0:T(8,128)S(1)}, f32[16,64,128]{2,1,0:T(8,128)}, u32[]{:S(2)}) %copy-start) | copy-done | bytes 524312
  1.7 0.0 copy-start.1
  1.7 1.0 %copy-done.1 = f32[15,64,128]{2,1,0:T(8,128)S(1)} copy-done((f32[15,64,128]{2,1,0:T(8,128)S(1)}, f32[15,64,128]{2,1,0:T(8,128)}, u32[]{:S(2)}) %copy-start.1) | copy-done | bytes 491544
  2.7 0.0 copy-start.2
  2.7 0.9 %copy-done.2 = f32[5,64,128]{2,1,0:T(8,128)S(1)} copy-done((f32[5,64,128]{2,1,0:T(8,128)S(1)}, f32[5,64,128]{2,1,0:T(8,128)}, u32[]{:S(2)}) %copy-start.2) | copy-done | bytes 163864
  3.6 0.0 copy-start.3
  3.6 0.9 %copy-done.3 = f32[5,64,128]{2,1,0:T(8,128)S(1)} copy-done((f32[5,64,128]{2,1,0:T(8,128)S(1)}, f32[5,64,128]{2,1,0:T(8,128)}, u32[]{:S(2)}) %copy-start.3) | copy-done | bytes 163864
  4.5 0.0 copy-start.4
  4.5 0.8 %copy-done.4 = f32[2,64,128]{2,1,0:T(8,128)S(1)} copy-done((f32[2,64,128]{2,1,0:T(8,128)S(1)}, f32[2,64,128]{2,1,0:T(8,128)}, u32[]{:S(2)}) %copy-start.4) | copy-done | bytes 65560
  5.4 0.0 copy-start.5
  5.4 0.8 %copy-done.5 = f32[2,64,128]{2,1,0:T(8,128)S(1)} copy-done((f32[2,64,128]{2,1,0:T(8,128)S(1)}, f32[2,64,128]{2,1,0:T(8,128)}, u32[]{:S(2)}) %copy-start.5) | copy-done | bytes 65560
  6.2 0.0 copy-start.6
  6.2 0.7 %copy-done.6 = s32[16]{0:T(128)S(1)} copy-done((s32[16]{0:T(128)S(1)}, s32[16]{0:T(128)}, u32[]{:S(2)}) %copy-start.6) | copy-done | bytes 88
  6.9 15.3 %ice_ocean.1 = (f32[16,64,128]{2,1,0:T(8,128)S(1)}, f32[2,64,128]{2,1,0:T(8,128)S(1)}, f32[2,64,128]{2,1,0:T(8,128)S(1)}) custom-call(s32[16]{0:T(128)S(1)} %copy-done.6, f32[2,64,128]{2,1,0:T(8,128)S(1)} %copy-done.4, f32[2,64,128]{2,1,0:T(8,128)S(1)} %copy-done.5, f32[5,64,128]{2,1,0:T(8,128)S(1)} %copy-done.2, f32[5,64,128]{2,1,0:T(8,128)S(1)} %copy-done.3, ...), custom_call_target="tpu_custom_call" | custom-call | tf_op jit(solution)/shard_map/ice_ocean/pallas_call | solution.py:274
  22.2 0.8 %copy.13 = f32[16,64,128]{2,1,0:T(8,128)} copy(f32[16,64,128]{2,1,0:T(8,128)S(1)} %get-tuple-element.6) | data formatting | bytes 1048576
  23.0 0.6 %copy.14 = f32[2,64,128]{2,1,0:T(8,128)} copy(f32[2,64,128]{2,1,0:T(8,128)S(1)} %get-tuple-element.7) | data formatting | bytes 131072
  23.6 0.6 %copy.15 = f32[2,64,128]{2,1,0:T(8,128)} copy(f32[2,64,128]{2,1,0:T(8,128)S(1)} %get-tuple-element.8) | data formatting | bytes 131072
Async XLA Ops:
  0.6 1.0 %copy-start = (f32[16,64,128]{2,1,0:T(8,128)S(1)}, f32[16,64,128]{2,1,0:T(8,128)}, u32[]{:S(2)}) copy-start(f32[16,64,128]{2,1,0:T(8,128)} %temp_hbm.1) | copy-start | bytes 1572868
  1.7 1.0 %copy-start.1 = (f32[15,64,128]{2,1,0:T(8,128)S(1)}, f32[15,64,128]{2,1,0:T(8,128)}, u32[]{:S(2)}) copy-start(f32[15,64,128]{2,1,0:T(8,128)} %kappa_hbm.1) | copy-start | bytes 1474564
  2.7 0.9 %copy-start.2 = (f32[5,64,128]{2,1,0:T(8,128)S(1)}, f32[5,64,128]{2,1,0:T(8,128)}, u32[]{:S(2)}) copy-start(f32[5,64,128]{2,1,0:T(8,128)} %area_hbm.1) | copy-start | bytes 491524
  3.6 0.9 %copy-start.3 = (f32[5,64,128]{2,1,0:T(8,128)S(1)}, f32[5,64,128]{2,1,0:T(8,128)}, u32[]{:S(2)}) copy-start(f32[5,64,128]{2,1,0:T(8,128)} %thick_hbm.1) | copy-start | bytes 491524
  4.5 0.8 %copy-start.4 = (f32[2,64,128]{2,1,0:T(8,128)S(1)}, f32[2,64,128]{2,1,0:T(8,128)}, u32[]{:S(2)}) copy-start(f32[2,64,128]{2,1,0:T(8,128)} %ocean_hbm.1) | copy-start | bytes 196612
  5.4 0.8 %copy-start.5 = (f32[2,64,128]{2,1,0:T(8,128)S(1)}, f32[2,64,128]{2,1,0:T(8,128)}, u32[]{:S(2)}) copy-start(f32[2,64,128]{2,1,0:T(8,128)} %wind_hbm.1) | copy-start | bytes 196612
  6.2 0.7 %copy-start.6 = (s32[16]{0:T(128)S(1)}, s32[16]{0:T(128)}, u32[]{:S(2)}) copy-start(s32[16]{0:T(128)} %mask.1) | copy-start | bytes 196

commit v2 on v1

--- a/solution.py
+++ b/solution.py
@@ -30,9 +30,9 @@
 
 
 def kernel(
-    slots, mask, ocean_hbm, wind_hbm, area_hbm, thick_hbm, temp_hbm, kappa_hbm,
+    slots, mask_hbm, ocean_hbm, wind_hbm, area_hbm, thick_hbm, temp_hbm, kappa_hbm,
     mixed_hbm, velocity_hbm, stress_hbm,
-    ocean, wind, area, thick, temp, kappa, fields, strips, mirrored, arrived,
+    mask, ocean, wind, area, thick, temp, kappa, fields, strips, mirrored, arrived,
     total_ref, weight_ref, first_ref, rows_ref, velocity, stress,
     in_sem, out_sem, send_sem, recv_sem,
 ):
@@ -49,7 +49,7 @@
     loads = [
         pltpu.make_async_copy(src, dst, in_sem.at[k])
         for k, (src, dst) in enumerate([
-            (area_hbm, area), (thick_hbm, thick), (ocean_hbm, ocean),
+            (mask_hbm, mask), (area_hbm, area), (thick_hbm, thick), (ocean_hbm, ocean),
             (wind_hbm, wind), (kappa_hbm, kappa), (temp_hbm, temp),
         ])
     ]
@@ -68,7 +68,7 @@
     def _():
         pl.semaphore_signal(barrier, inc=1, device_id=(ens, partner_west), device_id_type=MESH)
 
-    for load in loads[:4]:
+    for load in loads[:5]:
         load.wait()
 
     sub = lax.broadcasted_iota(jnp.int32, (8, 128), 0)
@@ -159,7 +159,7 @@
     for copy in copies:
         copy.start()
 
-    for load in loads[4:]:
+    for load in loads[5:]:
         load.wait()
     factor = None
     solved = None
@@ -278,9 +278,10 @@
                 jax.ShapeDtypeStruct(ocean_vel.shape, f32),
                 jax.ShapeDtypeStruct(ocean_vel.shape, f32),
             ),
-            in_specs=[pl.BlockSpec(memory_space=pltpu.SMEM)] + [any_spec] * 6,
+            in_specs=[any_spec] * 7,
             out_specs=(any_spec,) * 3,
             scratch_shapes=[
+                pltpu.SMEM(block_mask.shape, jnp.int32),
                 pltpu.VMEM((2, n, ny), f32),
                 pltpu.VMEM((2, n, ny), f32),
                 pltpu.VMEM((cats, n, ny), f32),
@@ -297,13 +298,13 @@
                 pltpu.VMEM((128, 2 * n), f32),
                 pltpu.VMEM((2, n, ny), f32),
                 pltpu.VMEM((2, n, ny), f32),
-                pltpu.SemaphoreType.DMA((6,)),
+                pltpu.SemaphoreType.DMA((7,)),
                 pltpu.SemaphoreType.DMA((6,)),
                 pltpu.SemaphoreType.DMA((7,)),
                 pltpu.SemaphoreType.DMA((7,)),
             ],
             compiler_params=pltpu.CompilerParams(
-                collective_id=0, has_side_effects=True, vmem_limit_bytes=24 * 1024 * 1024),
+                collective_id=0, has_side_effects=True, vmem_limit_bytes=60 * 1024 * 1024),
             name="ice_ocean",
         )(block_mask, ocean_vel, wind_stress, ice_area, ice_thick, temp, kappa)
 

time: 24.6 us -> 18.5 us (0.75)
  the two profiles are of different devices: /device:TPU:10 before, /device:TPU:0 now
where the time goes in v2:
time: 18.5 us; the launch traced here: 18.3 us
  Pallas kernels  14.3 us (77%)
  local copies, waits for them, and re-layouts  3.41 us (18%)
  between operations  0.65 us (4%)
    pallas_call x1, Pallas kernels, body(): pl.pallas_call(functools.partial(kernel, slots), out_shape=(jax.ShapeDtyp...  14.3 us
    unnamed x7, local copies, waits for them, and re-layouts  3.41 us

profile of v2, /device:TPU:0, one launch (start us, length us, event | category | flops | bytes accessed | tf_op | source)
XLA Modules:
  0.0 18.3 jit_solution(5826898979818022199)
XLA Ops:
  0.6 14.3 %ice_ocean.1 = (f32[16,64,128]{2,1,0:T(8,128)}, f32[2,64,128]{2,1,0:T(8,128)}, f32[2,64,128]{2,1,0:T(8,128)}) custom-call(s32[16]{0:T(128)} %mask_hbm.1, f32[2,64,128]{2,1,0:T(8,128)} %ocean_hbm.1, f32[2,64,128]{2,1,0:T(8,128)} %wind_hbm.1, f32[5,64,128]{2,1,0:T(8,128)} %area_hbm.1, f32[5,64,128]{2,1,0:T(8,128)} %thick_hbm.1, f32[16,64,128]{2,1,0:T(8,128)} %temp_hbm.1, ...), custom_call_target="tpu_custom_call" | custom-call | tf_op jit(solution)/shard_map/ice_ocean/pallas_call | solution.py:274
  14.9 0.0 copy-start.1
  14.9 1.9 %copy.13 = f32[16,64,128]{2,1,0:T(8,128)} copy(f32[16,64,128]{2,1,0:T(8,128)} %get-tuple-element.6) | data formatting | bytes 1048576
  16.8 0.0 copy-done.1
  16.9 0.0 copy-start
  16.9 0.6 %copy.14 = f32[2,64,128]{2,1,0:T(8,128)} copy(f32[2,64,128]{2,1,0:T(8,128)S(1)} %copy-done.1) | data formatting | bytes 131072
  17.5 0.2 %copy-done = f32[2,64,128]{2,1,0:T(8,128)S(1)} copy-done((f32[2,64,128]{2,1,0:T(8,128)S(1)}, f32[2,64,128]{2,1,0:T(8,128)}, u32[]{:S(2)}) %copy-start) | copy-done | bytes 65560
  17.7 0.6 %copy.15 = f32[2,64,128]{2,1,0:T(8,128)} copy(f32[2,64,128]{2,1,0:T(8,128)S(1)} %copy-done) | data formatting | bytes 131072
Async XLA Ops:
  14.9 1.9 %copy-start.1 = (f32[2,64,128]{2,1,0:T(8,128)S(1)}, f32[2,64,128]{2,1,0:T(8,128)}, u32[]{:S(2)}) copy-start(f32[2,64,128]{2,1,0:T(8,128)} %get-tuple-element.7) | copy-start | bytes 196612
  16.9 0.9 %copy-start = (f32[2,64,128]{2,1,0:T(8,128)S(1)}, f32[2,64,128]{2,1,0:T(8,128)}, u32[]{:S(2)}) copy-start(f32[2,64,128]{2,1,0:T(8,128)} %get-tuple-element.8) | copy-start | bytes 196612

commit v3 on v2

--- a/solution.py
+++ b/solution.py
@@ -31,13 +31,17 @@
 
 def kernel(
     slots, mask_hbm, ocean_hbm, wind_hbm, area_hbm, thick_hbm, temp_hbm, kappa_hbm,
-    mixed_hbm, velocity_hbm, stress_hbm,
+    result,
     mask, ocean, wind, area, thick, temp, kappa, fields, strips, mirrored, arrived,
-    total_ref, weight_ref, first_ref, rows_ref, velocity, stress,
-    in_sem, out_sem, send_sem, recv_sem,
+    total_ref, weight_ref, first_ref, rows_ref,
+    in_sem, send_sem, recv_sem,
 ):
     n = ocean.shape[1]
     levels = temp.shape[0]
+    solved_out = result.at[pl.ds(0, levels)]
+    factor_out = result.at[pl.ds(levels, levels - 1)]
+    velocity = result.at[pl.ds(2 * levels - 1, 2)]
+    stress = result.at[pl.ds(2 * levels + 1, 2)]
     width = n // mask.shape[0]
     ens, here = lax.axis_index("ens"), lax.axis_index("gx")
     east = lax.rem(here + 1, slots)
@@ -176,14 +180,14 @@
             factor = above * inverse
             solved = target * inverse
             if level < levels - 1:
-                kappa[level] = carried
+                factor_out[level] = carried
             carried = factor
-            temp[level] = solved
+            solved_out[level] = solved
         else:
-            kappa[0] = carried
+            factor_out[0] = carried
             inverse = 1.0 / pivot
             first_ref[...] = inverse
-            temp[0] = target * inverse
+            solved_out[0] = target * inverse
 
     @pl.when(partner_west != here)
     def _():
@@ -241,22 +245,29 @@
         drag = scale * (w - ocean[comp])
         stress[comp] = drag
         source = source + drag * ocean[comp]
+    solved_out[0] = solved_out[0] + first_ref[...] * source
+
+
+def back_kernel(middle, mixed_hbm, velocity_hbm, stress_hbm, mixed, out_sem):
+    levels = mixed.shape[0]
+    velocity = middle.at[pl.ds(2 * levels - 1, 2)]
+    stress = middle.at[pl.ds(2 * levels + 1, 2)]
     stores = [
         pltpu.make_async_copy(velocity, velocity_hbm, out_sem.at[0]),
         pltpu.make_async_copy(stress, stress_hbm, out_sem.at[1]),
     ]
     for store in stores:
         store.start()
-    level_value = temp[0] + first_ref[...] * source
-    temp[0] = level_value
+    value = middle[0]
+    mixed[0] = value
     quarter = levels // 4
     for level in range(1, levels):
-        level_value = temp[level] + kappa[level - 1] * level_value
-        temp[level] = level_value
+        value = middle[level] + middle[levels + level - 1] * value
+        mixed[level] = value
         if level % quarter == quarter - 1:
             part = pl.ds(level - quarter + 1, quarter)
             store = pltpu.make_async_copy(
-                temp.at[part], mixed_hbm.at[part], out_sem.at[2 + level // quarter])
+                mixed.at[part], mixed_hbm.at[part], out_sem.at[2 + level // quarter])
             store.start()
             stores.append(store)
     for store in stores:
@@ -269,17 +280,16 @@
     def body(ocean_vel, wind_stress, ice_area, ice_thick, block_mask, temp, kappa):
         n, ny = ocean_vel.shape[1:]
         levels, cats = temp.shape[0], ice_area.shape[0]
-        any_spec = pl.BlockSpec(memory_space=pl.ANY)
         f32 = jnp.float32
-        return pl.pallas_call(
+        hbm = pl.BlockSpec(memory_space=pltpu.HBM)
+        vmem = pl.BlockSpec(memory_space=pltpu.VMEM)
+        column = jax.ShapeDtypeStruct(temp.shape, f32)
+        pair = jax.ShapeDtypeStruct(ocean_vel.shape, f32)
+        middle = pl.pallas_call(
             functools.partial(kernel, slots),
-            out_shape=(
-                jax.ShapeDtypeStruct(temp.shape, f32),
-                jax.ShapeDtypeStruct(ocean_vel.shape, f32),
-                jax.ShapeDtypeStruct(ocean_vel.shape, f32),
-            ),
-            in_specs=[any_spec] * 7,
-            out_specs=(any_spec,) * 3,
+            out_shape=jax.ShapeDtypeStruct((2 * levels + 3, n, ny), f32),
+            in_specs=[hbm] * 7,
+            out_specs=vmem,
             scratch_shapes=[
                 pltpu.SMEM(block_mask.shape, jnp.int32),
                 pltpu.VMEM((2, n, ny), f32),
@@ -296,17 +306,23 @@
                 pltpu.VMEM((n, ny), f32),
                 pltpu.VMEM((n, ny), f32),
                 pltpu.VMEM((128, 2 * n), f32),
-                pltpu.VMEM((2, n, ny), f32),
-                pltpu.VMEM((2, n, ny), f32),
                 pltpu.SemaphoreType.DMA((7,)),
-                pltpu.SemaphoreType.DMA((6,)),
                 pltpu.SemaphoreType.DMA((7,)),
                 pltpu.SemaphoreType.DMA((7,)),
             ],
             compiler_params=pltpu.CompilerParams(
-                collective_id=0, has_side_effects=True, vmem_limit_bytes=60 * 1024 * 1024),
+                collective_id=0, has_side_effects=True, vmem_limit_bytes=60817408),
             name="ice_ocean",
         )(block_mask, ocean_vel, wind_stress, ice_area, ice_thick, temp, kappa)
+        return pl.pallas_call(
+            back_kernel,
+            out_shape=(column, pair, pair),
+            in_specs=[vmem],
+            out_specs=(hbm,) * 3,
+            scratch_shapes=[pltpu.VMEM(temp.shape, f32), pltpu.SemaphoreType.DMA((6,))],
+            compiler_params=pltpu.CompilerParams(vmem_limit_bytes=10 * 1024 * 1024),
+            name="back_substitution",
+        )(middle)
 
     split = P("ens", "gx", None)
     return jax.shard_map(

time: 18.5 us -> 17.3 us (0.935)
  local copies, waits for them, and re-layouts: 3.41 us -> 1.25 us
  Pallas kernels: 14.3 us -> 15.3 us
    unnamed x7 -> x2, local copies, waits for them, and re-layouts: 3.41 us -> 1.25 us
    pallas_call x1 -> x2, Pallas kernels: 14.3 us -> 15.3 us  [the longest x1 14.4 us: body(): pl.pallas_call(functools.partial(kernel, slots), out_shape=jax.ShapeDtype...]
where the time goes in v3:
time: 17.3 us; the launch traced here: 17.2 us
  Pallas kernels  15.3 us (88%)
  local copies, waits for them, and re-layouts  1.25 us (7%)
  between operations  0.65 us (4%)
    pallas_call x1, Pallas kernels, body(): pl.pallas_call(functools.partial(kernel, slots), out_shape=jax.ShapeDtype...  14.4 us
    unnamed x2, local copies, waits for them, and re-layouts  1.25 us
    pallas_call x1, Pallas kernels, body(): pl.pallas_call(back_kernel, out_shape=(column, pair, pair), in_specs=[vme...  0.88 us

profile of v3, /device:TPU:0, one launch (start us, length us, event | category | flops | bytes accessed | tf_op | source)
XLA Modules:
  0.0 17.2 jit_solution(727140745184520222)
XLA Ops:
  0.6 14.4 %ice_ocean.1.middle = f32[35,64,128]{2,1,0:T(8,128)} custom-call(s32[16]{0:T(128)} %mask_hbm.1, f32[2,64,128]{2,1,0:T(8,128)} %ocean_hbm.1, f32[2,64,128]{2,1,0:T(8,128)} %wind_hbm.1, f32[5,64,128]{2,1,0:T(8,128)} %area_hbm.1, f32[5,64,128]{2,1,0:T(8,128)} %thick_hbm.1, f32[16,64,128]{2,1,0:T(8,128)} %temp_hbm.1, f32[15,64,128]{2,1,0:T(8,128)} %kappa_hbm.1), custom_call_target="tpu_custom_call" | custom-call | tf_op jit(solution)/shard_map/ice_ocean/pallas_call | solution.py:288
  15.0 0.0 copy-start
  15.0 1.2 %copy-done = f32[35,64,128]{2,1,0:T(8,128)S(1)} copy-done((f32[35,64,128]{2,1,0:T(8,128)S(1)}, f32[35,64,128]{2,1,0:T(8,128)}, u32[]{:S(2)}) %copy-start) | copy-done | bytes 1146904
  16.3 0.9 %back_substitution.1 = (f32[16,64,128]{2,1,0:T(8,128)}, f32[2,64,128]{2,1,0:T(8,128)}, f32[2,64,128]{2,1,0:T(8,128)}) custom-call(f32[35,64,128]{2,1,0:T(8,128)S(1)} %copy-done), custom_call_target="tpu_custom_call" | custom-call | tf_op jit(solution)/shard_map/back_substitution/pallas_call | solution.py:317
Async XLA Ops:
  15.0 1.3 %copy-start = (f32[35,64,128]{2,1,0:T(8,128)S(1)}, f32[35,64,128]{2,1,0:T(8,128)}, u32[]{:S(2)}) copy-start(f32[35,64,128]{2,1,0:T(8,128)} %ice_ocean.1.middle) | copy-start | bytes 3440644

commit v4 on v3

--- a/solution.py
+++ b/solution.py
@@ -32,7 +32,7 @@
 def kernel(
     slots, mask_hbm, ocean_hbm, wind_hbm, area_hbm, thick_hbm, temp_hbm, kappa_hbm,
     result,
-    mask, ocean, wind, area, thick, temp, kappa, fields, strips, mirrored, arrived,
+    mask, ocean, wind, area, thick, temp, kappa, fields, strips, mirrored, arrived, packed, corners,
     total_ref, weight_ref, first_ref, rows_ref,
     in_sem, send_sem, recv_sem,
 ):
@@ -118,12 +118,22 @@
     forward = jnp.concatenate([top[:HALO] for top in tops], 0)
     backward = jnp.concatenate(
         [(-top[HALO:] if k < 4 else top[HALO:]) for k, top in enumerate(tops)], 0)
-    strips[...] = jnp.dot(
-        forward, place, precision=HIGH, preferred_element_type=jnp.float32
-    ).reshape(FIELDS, HALO, 2 * n)
-    mirrored[...] = jnp.dot(
-        backward, place_back, precision=HIGH, preferred_element_type=jnp.float32
-    ).reshape(FIELDS, HALO, 2 * n)
+    plain = jnp.dot(forward, place, precision=HIGH, preferred_element_type=jnp.float32)
+    plain = plain.reshape(FIELDS, HALO, 2 * n)
+    strips[...] = plain
+    turned = jnp.dot(backward, place_back, precision=HIGH, preferred_element_type=jnp.float32)
+    turned = turned.reshape(FIELDS, HALO, 2 * n)
+    mirrored[...] = turned
+    slot = lax.broadcasted_iota(jnp.int32, (HALO, 128), 1)
+    for index, (block, base) in enumerate(
+        [(plain, 0), (plain, n - HALO), (turned, 0), (turned, n - HALO)]
+    ):
+        tile = jnp.zeros((HALO, 128), jnp.float32)
+        for k in range(FIELDS):
+            shift = (HALO * k - base) % (2 * n)
+            moved = pltpu.roll(block[k], shift, 1) if shift else block[k]
+            tile = jnp.where(slot >= HALO * k, moved[:, :128], tile)
+        packed[index] = tile
 
     others = (partner_east != here).astype(jnp.int32) + (partner_west != here).astype(jnp.int32)
     pl.semaphore_wait(barrier, 3 + others)
@@ -135,14 +145,14 @@
 
     first, last = pl.ds(HALO, HALO), pl.ds(n, HALO)
     copies = [
-        remote(mirrored, arrived.at[2], 2, partner),
-        remote(strips, arrived.at[0], 0, east),
-        remote(strips, arrived.at[1], 1, west),
+        remote(mirrored, arrived, 2, partner),
+        remote(packed.at[1], corners.at[1], 0, east),
+        remote(packed.at[0], corners.at[0], 1, west),
         remote(fields.at[:, last, :], fields.at[:, pl.ds(0, HALO), :], 5, east),
         remote(fields.at[:, first, :], fields.at[:, pl.ds(HALO + n, HALO), :], 6, west),
     ]
-    to_west = remote(mirrored, arrived.at[3], 3, partner_west)
-    to_east = remote(mirrored, arrived.at[4], 4, partner_east)
+    to_west = remote(packed.at[2], corners.at[2], 3, partner_west)
+    to_east = remote(packed.at[3], corners.at[3], 4, partner_east)
 
     @pl.when(partner_west != here)
     def _():
@@ -150,7 +160,7 @@
 
     @pl.when(partner_west == here)
     def _():
-        arrived[3] = mirrored[...]
+        corners[2] = packed[2]
 
     @pl.when(partner_east != here)
     def _():
@@ -158,7 +168,7 @@
 
     @pl.when(partner_east == here)
     def _():
-        arrived[4] = mirrored[...]
+        corners[3] = packed[3]
 
     for copy in copies:
         copy.start()
@@ -201,12 +211,24 @@
         copy.wait()
 
     lane = lax.broadcasted_iota(jnp.int32, (HALO, 2 * n), 1)
+    tiles = []
+    for index in range(4):
+        tile = corners[index]
+        if 2 * n > 128:
+            tile = jnp.concatenate([tile, jnp.zeros((HALO, 2 * n - 128), jnp.float32)], 1)
+        tiles.append(tile)
+
+    def unpack(index, base, k):
+        shift = (base - HALO * k) % (2 * n)
+        return pltpu.roll(tiles[index], shift, 1) if shift else tiles[index]
+
     strip = []
     for k in range(FIELDS):
-        south = jnp.where(
-            lane >= n, strips[k], jnp.where(lane >= n // 2, arrived[0, k], arrived[1, k]))
+        low, high, low_turned, high_turned = [
+            unpack(index, (index % 2) * (n - HALO), k) for index in range(4)]
+        south = jnp.where(lane >= n, strips[k], jnp.where(lane >= n // 2, high, low))
         north = jnp.where(
-            lane >= n, arrived[2, k], jnp.where(lane >= n // 2, arrived[4, k], arrived[3, k]))
+            lane >= n, arrived[k], jnp.where(lane >= n // 2, high_turned, low_turned))
         strip.append(jnp.concatenate([south, north], 0))
     u, v, fu, fv, half = strip
     for count in range(ITERS):
@@ -301,7 +323,9 @@
                 pltpu.VMEM((FIELDS, n + 2 * HALO, ny), f32),
                 pltpu.VMEM((FIELDS, HALO, 2 * n), f32),
                 pltpu.VMEM((FIELDS, HALO, 2 * n), f32),
-                pltpu.VMEM((5, FIELDS, HALO, 2 * n), f32),
+                pltpu.VMEM((FIELDS, HALO, 2 * n), f32),
+                pltpu.VMEM((4, HALO, 128), f32),
+                pltpu.VMEM((4, HALO, 128), f32),
                 pltpu.VMEM((n, ny), f32),
                 pltpu.VMEM((n, ny), f32),
                 pltpu.VMEM((n, ny), f32),

time: 17.3 us -> 16.1 us (0.931)
  Pallas kernels: 15.3 us -> 14 us
    pallas_call x1, Pallas kernels: 14.4 us -> 13.1 us  [body(): pl.pallas_call(functools.partial(kernel, slots), out_shape=jax.ShapeDtype...]
where the time goes in v4:
time: 16.1 us; the launch traced here: 15.9 us
  Pallas kernels  14 us (87%)
  local copies, waits for them, and re-layouts  1.25 us (8%)
  between operations  0.65 us (4%)
    pallas_call x1, Pallas kernels, body(): pl.pallas_call(functools.partial(kernel, slots), out_shape=jax.ShapeDtype...  13.1 us
    unnamed x2, local copies, waits for them, and re-layouts  1.25 us
    pallas_call x1, Pallas kernels, body(): pl.pallas_call(back_kernel, out_shape=(column, pair, pair), in_specs=[vme...  0.88 us

profile of v4, /device:TPU:0, one launch (start us, length us, event | category | flops | bytes accessed | tf_op | source)
XLA Modules:
  0.0 15.9 jit_solution(2745839331313268159)
XLA Ops:
  0.6 13.1 %ice_ocean.1.middle = f32[35,64,128]{2,1,0:T(8,128)} custom-call(s32[16]{0:T(128)} %mask_hbm.1, f32[2,64,128]{2,1,0:T(8,128)} %ocean_hbm.1, f32[2,64,128]{2,1,0:T(8,128)} %wind_hbm.1, f32[5,64,128]{2,1,0:T(8,128)} %area_hbm.1, f32[5,64,128]{2,1,0:T(8,128)} %thick_hbm.1, f32[16,64,128]{2,1,0:T(8,128)} %temp_hbm.1, f32[15,64,128]{2,1,0:T(8,128)} %kappa_hbm.1), custom_call_target="tpu_custom_call" | custom-call | tf_op jit(solution)/shard_map/ice_ocean/pallas_call | solution.py:310
  13.8 0.0 copy-start
  13.8 1.2 %copy-done = f32[35,64,128]{2,1,0:T(8,128)S(1)} copy-done((f32[35,64,128]{2,1,0:T(8,128)S(1)}, f32[35,64,128]{2,1,0:T(8,128)}, u32[]{:S(2)}) %copy-start) | copy-done | bytes 1146904
  15.0 0.9 %back_substitution.1 = (f32[16,64,128]{2,1,0:T(8,128)}, f32[2,64,128]{2,1,0:T(8,128)}, f32[2,64,128]{2,1,0:T(8,128)}) custom-call(f32[35,64,128]{2,1,0:T(8,128)S(1)} %copy-done), custom_call_target="tpu_custom_call" | custom-call | tf_op jit(solution)/shard_map/back_substitution/pallas_call | solution.py:341
Async XLA Ops:
  13.8 1.3 %copy-start = (f32[35,64,128]{2,1,0:T(8,128)S(1)}, f32[35,64,128]{2,1,0:T(8,128)}, u32[]{:S(2)}) copy-start(f32[35,64,128]{2,1,0:T(8,128)} %ice_ocean.1.middle) | copy-start | bytes 3440644

commit v5 on v4

--- a/solution.py
+++ b/solution.py
@@ -123,7 +123,10 @@
     strips[...] = plain
     turned = jnp.dot(backward, place_back, precision=HIGH, preferred_element_type=jnp.float32)
     turned = turned.reshape(FIELDS, HALO, 2 * n)
-    mirrored[...] = turned
+    half_lane = lax.broadcasted_iota(jnp.int32, (HALO, 2 * n), 1)
+    for pair in range(3):
+        mirrored[pair] = jnp.where(
+            half_lane < n, turned[2 * pair], turned[min(2 * pair + 1, FIELDS - 1)])
     slot = lax.broadcasted_iota(jnp.int32, (HALO, 128), 1)
     for index, (block, base) in enumerate(
         [(plain, 0), (plain, n - HALO), (turned, 0), (turned, n - HALO)]
@@ -226,9 +229,12 @@
     for k in range(FIELDS):
         low, high, low_turned, high_turned = [
             unpack(index, (index % 2) * (n - HALO), k) for index in range(4)]
+        opposite = arrived[k // 2]
+        if k % 2 == 0 and k < FIELDS - 1:
+            opposite = pltpu.roll(opposite, n, 1)
         south = jnp.where(lane >= n, strips[k], jnp.where(lane >= n // 2, high, low))
         north = jnp.where(
-            lane >= n, arrived[k], jnp.where(lane >= n // 2, high_turned, low_turned))
+            lane >= n, opposite, jnp.where(lane >= n // 2, high_turned, low_turned))
         strip.append(jnp.concatenate([south, north], 0))
     u, v, fu, fv, half = strip
     for count in range(ITERS):
@@ -322,8 +328,8 @@
                 pltpu.VMEM((levels - 1, n, ny), f32),
                 pltpu.VMEM((FIELDS, n + 2 * HALO, ny), f32),
                 pltpu.VMEM((FIELDS, HALO, 2 * n), f32),
-                pltpu.VMEM((FIELDS, HALO, 2 * n), f32),
-                pltpu.VMEM((FIELDS, HALO, 2 * n), f32),
+                pltpu.VMEM((3, HALO, 2 * n), f32),
+                pltpu.VMEM((3, HALO, 2 * n), f32),
                 pltpu.VMEM((4, HALO, 128), f32),
                 pltpu.VMEM((4, HALO, 128), f32),
                 pltpu.VMEM((n, ny), f32),

time: 16.1 us -> 15.8 us (0.981)
  Pallas kernels: 14 us -> 13.8 us
    pallas_call x1, Pallas kernels: 13.1 us -> 12.9 us  [body(): pl.pallas_call(functools.partial(kernel, slots), out_shape=jax.ShapeDtype...]
where the time goes in v5:
time: 15.8 us; the launch traced here: 15.7 us
  Pallas kernels  13.8 us (87%)
  local copies, waits for them, and re-layouts  1.25 us (8%)
  between operations  0.65 us (4%)
    pallas_call x1, Pallas kernels, body(): pl.pallas_call(functools.partial(kernel, slots), out_shape=jax.ShapeDtype...  12.9 us
    unnamed x2, local copies, waits for them, and re-layouts  1.25 us
    pallas_call x1, Pallas kernels, body(): pl.pallas_call(back_kernel, out_shape=(column, pair, pair), in_specs=[vme...  0.88 us

profile of v5, /device:TPU:0, one launch (start us, length us, event | category | flops | bytes accessed | tf_op | source)
XLA Modules:
  0.0 15.7 jit_solution(17099766870370158760)
XLA Ops:
  0.6 12.9 %ice_ocean.1.middle = f32[35,64,128]{2,1,0:T(8,128)} custom-call(s32[16]{0:T(128)} %mask_hbm.1, f32[2,64,128]{2,1,0:T(8,128)} %ocean_hbm.1, f32[2,64,128]{2,1,0:T(8,128)} %wind_hbm.1, f32[5,64,128]{2,1,0:T(8,128)} %area_hbm.1, f32[5,64,128]{2,1,0:T(8,128)} %thick_hbm.1, f32[16,64,128]{2,1,0:T(8,128)} %temp_hbm.1, f32[15,64,128]{2,1,0:T(8,128)} %kappa_hbm.1), custom_call_target="tpu_custom_call" | custom-call | tf_op jit(solution)/shard_map/ice_ocean/pallas_call | solution.py:316
  13.5 0.0 copy-start
  13.5 1.2 %copy-done = f32[35,64,128]{2,1,0:T(8,128)S(1)} copy-done((f32[35,64,128]{2,1,0:T(8,128)S(1)}, f32[35,64,128]{2,1,0:T(8,128)}, u32[]{:S(2)}) %copy-start) | copy-done | bytes 1146904
  14.8 0.9 %back_substitution.1 = (f32[16,64,128]{2,1,0:T(8,128)}, f32[2,64,128]{2,1,0:T(8,128)}, f32[2,64,128]{2,1,0:T(8,128)}) custom-call(f32[35,64,128]{2,1,0:T(8,128)S(1)} %copy-done), custom_call_target="tpu_custom_call" | custom-call | tf_op jit(solution)/shard_map/back_substitution/pallas_call | solution.py:347
Async XLA Ops:
  13.5 1.3 %copy-start = (f32[35,64,128]{2,1,0:T(8,128)S(1)}, f32[35,64,128]{2,1,0:T(8,128)}, u32[]{:S(2)}) copy-start(f32[35,64,128]{2,1,0:T(8,128)} %ice_ocean.1.middle) | copy-start | bytes 3440644
